TPU v7x, 32 devices: a whole 2x2x4 slice. The times are simulated.
32 devices in a mesh: chan: 16 (over z, x, core), rows: 2 (over y).
Axes of the slice: x: 2, y: 2, z: 4, core: 2. Of those that a mesh axis runs over, the one named last changes fastest.
Arguments:
- inputs: bfloat16 [1, 2, 256, 2048], P(None, 'rows', None, 'chan'), may hold values from -6 to 6
- weights: bfloat16 [3, 3, 2048, 2048], P(None, None, 'chan'), may hold values from -0.0625 to 0.0625
- cotangent: bfloat16 [1, 2, 256, 2048], P(None, 'rows', None, 'chan'), may hold values from -6 to 6
Outputs:
- outputs: bfloat16 [1, 2, 256, 2048], P(None, 'rows', None, 'chan')
- input_grad: bfloat16 [1, 2, 256, 2048], P(None, 'rows', None, 'chan')
- weight_grad: float32 [3, 3, 2048, 2048], P(None, None, 'chan', 'rows')
All inputs are finite; a program needn't handle non-finite values.
Results may differ from a plain program's by a relative error of at most 0.001.
Values may be sent and summed in bfloat16 or wider, within the bound.
A program may use at most 128 MiB of HBM per device.

v0:
```python
import jax
import jax.numpy as jnp
from jax import lax
from jax.sharding import PartitionSpec as P


def with_halo(array, sides, width):
    for axis, dim in sides:
        devices, length = (lax.axis_size(axis), array.shape[dim])
        up = [(i, (i + 1) % devices) for i in range(devices - 1)]
        down = [(j, i) for i, j in up]
        last = lax.slice_in_dim(array, length - width, length, axis=dim)
        initial = lax.slice_in_dim(array, 0, width, axis=dim)
        before = lax.ppermute(last, axis, up)
        after = lax.ppermute(initial, axis, down)
        array = jnp.concatenate([before, array, after], axis=dim)
    return array


def unfold(padded, height, breadth):
    taps = [
        padded[:, row_off : row_off + height, col_off : col_off + breadth, :]
        for row_off in range(3)
        for col_off in range(3)
    ]
    stacked = jnp.concatenate(taps, axis=3)
    return stacked.reshape(-1, stacked.shape[3])


def pad_columns(rimmed):
    return jnp.pad(rimmed, ((0, 0), (0, 0), (1, 1), (0, 0)))


def on_device(inputs, weights, cotangent):
    batches = inputs.shape[0]
    height = inputs.shape[1]
    breadth = inputs.shape[2]
    local_ch = inputs.shape[3]
    channels = weights.shape[3]
    pixels = batches * height * breadth
    contract_first = (((0,), (1,)), ((), ()))
    rimmed = with_halo(inputs, (("rows", 1),), 1)
    columns = unfold(pad_columns(rimmed), height, breadth)
    matrix = weights.reshape(9 * local_ch, channels)
    block = matrix
    conv_out = lax.psum_scatter(
        lax.dot_general(block, columns, contract_first, preferred_element_type=jnp.float32),
        "chan",
        scatter_dimension=0,
        tiled=True,
    )
    outputs = conv_out.T.reshape(batches, height, breadth, local_ch).astype(jnp.bfloat16)
    grad_rimmed = with_halo(cotangent, (("rows", 1),), 1)
    flipped = jnp.transpose(weights[::-1, ::-1], (2, 0, 1, 3))
    piece = lax.all_gather(grad_rimmed, "chan", axis=3, tiled=True)
    count = piece.shape[3]
    grad_cols = unfold(pad_columns(piece), height, breadth)
    block = flipped.reshape(local_ch, 9 * count)
    data_sum = lax.dot_general(
        block, grad_cols, (((1,), (1,)), ((), ())), preferred_element_type=jnp.float32
    )
    inner = piece[:, 1 : height + 1].reshape(pixels, count)
    update = lax.dot_general(
        columns, inner, (((0,), (0,)), ((), ())), preferred_element_type=jnp.float32
    )
    filter_sum = update
    data_sum, filter_sum = (data_sum, filter_sum)
    input_grad = data_sum.T.reshape(batches, height, breadth, local_ch).astype(jnp.bfloat16)
    total_pixels = pixels * lax.axis_size("rows")
    scaled = (filter_sum / jnp.sqrt(jnp.float32(total_pixels))).reshape(3, 3, local_ch, channels)
    weight_grad = lax.psum_scatter(scaled, "rows", scatter_dimension=3, tiled=True)
    return (outputs, input_grad, weight_grad)


def solution(mesh):
    in_specs = (
        P(None, "rows", None, "chan"),
        P(None, None, "chan", None),
        P(None, "rows", None, "chan"),
    )
    out_specs = (
        P(None, "rows", None, "chan"),
        P(None, "rows", None, "chan"),
        P(None, None, "chan", "rows"),
    )
    return jax.shard_map(
        on_device, mesh=mesh, in_specs=in_specs, out_specs=out_specs, check_vma=False
    )
```

profile of v0, /device:TPU:0, one launch (start us, length us, event | category | flops | bytes accessed | tf_op | source)
XLA Modules:
  0.0 250.3 jit_solution(17633905704568887612)
XLA Ops:
  7.2 4.9 %collective-permute-start.2 = (bf16[1,1,256,128]{3,2,1,0:T(8,128)(2,1)}, bf16[1,1,256,128]{3,2,1,0:T(8,128)(2,1)S(1)}, u32[]{:S(2)}, u32[]{:S(2)}) collective-permute-start(bf16[1,1,256,128]{3,2,1,0:T(8,128)(2,1)} %param.5), channel_id=1, source_target_pairs={{0,1},{2,3},{4,5},{6,7},{8,9},{10,11},{12,13},{14,15},{16,17},{18,... | collective-permute-start | bytes 196616 | tf_op jit(solution)/shard_map/ppermute | solution.py:14
  12.1 1.3 collective-permute-start.3
  13.4 0.9 collective-permute-done.2
  14.3 4.2 %collective-permute-done.3 = bf16[1,1,256,128]{3,2,1,0:T(8,128)(2,1)S(1)} collective-permute-done((bf16[1,1,256,128]{3,2,1,0:T(8,128)(2,1)}, bf16[1,1,256,128]{3,2,1,0:T(8,128)(2,1)S(1)}, u32[]{:S(2)}, u32[]{:S(2)}) %collective-permute-start.3) | collective-permute-done | bytes 65568 | tf_op jit(solution)/shard_map/ppermute | solution.py:15
  18.5 1.5 pad_maximum_fusion
  20.1 1.7 collective-permute-start
  21.8 1.3 collective-permute-start.1
  23.1 0.9 collective-permute-done
  24.0 4.2 %collective-permute-done.1 = bf16[1,1,256,128]{3,2,1,0:T(8,128)(2,1)S(1)} collective-permute-done((bf16[1,1,256,128]{3,2,1,0:T(8,128)(2,1)}, bf16[1,1,256,128]{3,2,1,0:T(8,128)(2,1)S(1)}, u32[]{:S(2)}, u32[]{:S(2)}) %collective-permute-start.1) | collective-permute-done | bytes 65568 | tf_op jit(solution)/shard_map/ppermute | solution.py:15
  28.1 0.9 fusion.23
  29.1 0.9 constant_dynamic-update-slice_fusion.1
  30.1 5.2 %convolution_bitcast_fusion = f32[2048,256]{0,1:T(8,128)} fusion(bf16[1152,2048]{1,0:T(8,128)(2,1)} %bitcast.34, bf16[1,1,256,1152]{3,2,1,0:T(8,128)(2,1)S(1)} %slice_dynamic-update-slice_fusion.3), kind=kOutput, calls=%fused_computation.3 | convolution fusion | flops 1207959552 | bytes 7405568 | tf_op jit(solution)/shard_map/dot_general | solution.py:47
  35.4 32.2 %all-gather.2.cloned.1.call-done = bf16[1,3,256,2048]{3,2,1,0:T(8,128)(2,1)} async-done(((bf16[1,3,256,128]{3,2,1,0:T(8,128)(2,1)}), bf16[1,3,256,2048]{3,2,1,0:T(8,128)(2,1)}) %all-gather.2.cloned.1.call-update) | async-done | bytes 3145744 | tf_op jit(solution)/shard_map/all_gather | solution.py:55
  67.7 6.3 %convolution_multiply_fusion = f32[1152,2048]{1,0:T(8,128)} fusion(bf16[1,3,256,2048]{3,2,1,0:T(8,128)(2,1)} %all-gather.2.cloned.1.call-done, bf16[1,1,256,1152]{3,2,1,0:T(8,128)(2,1)S(1)} %slice_dynamic-update-slice_fusion.3), kind=kOutput, calls=%fused_computation | convolution fusion | flops 1210318848 | bytes 11075584 | tf_op jit(solution)/shard_map/dot_general | solution.py:63
  74.0 6.9 %copy.6 = bf16[3,3,128,2048]{2,3,1,0:T(8,128)(2,1)} copy(bf16[3,3,128,2048]{3,2,1,0:T(8,128)(2,1)} %param.4) | data formatting | bytes 9437184 | tf_op args[1]
  80.9 5.0 %rev.3 = bf16[3,3,128,2048]{2,3,1,0:T(8,128)(2,1)} reverse(bf16[3,3,128,2048]{2,3,1,0:T(8,128)(2,1)} %copy.6), dimensions={0,1} | reverse | bytes 9437184 | tf_op jit(solution)/shard_map/rev | solution.py:54
  85.9 45.3 %reduce-scatter.3.cloned.1.call-done = f32[128,256]{0,1:T(8,128)} async-done(((f32[2048,256]{0,1:T(8,128)}), f32[128,256]{0,1:T(8,128)}) %reduce-scatter.3.cloned.1.call-update) | async-done | bytes 131088 | tf_op jit(solution)/shard_map/reduce_scatter | solution.py:46
  131.2 1.5 convert_bitcast_fusion
  132.7 0.3 fusion.8
  133.3 0.3 fusion.10
  134.0 0.3 fusion.12
  134.6 1.2 slice-done
  136.0 3.2 %fusion.5 = bf16[1,1,256,128]{3,2,1,0:T(8,128)(2,1)} fusion(bf16[128,18432]{0,1:T(8,128)(2,1)S(1)} %bitcast.33, bf16[1,1,256,18432]{3,2,1,0:T(8,128)(2,1)S(1)} %fusion.13), kind=kOutput, calls=%fused_computation.11 | convolution fusion | flops 1207992320 | bytes 14221312 | tf_op jit(solution)/shard_map/dot_general | solution.py:59
  139.2 104.6 %reduce-scatter.5.cloned.1.call-done = f32[3,3,128,1024]{3,2,1,0:T(8,128)} async-done(((f32[3,3,128,2048]{3,2,1,0:T(8,128)}), f32[3,3,128,1024]{3,2,1,0:T(8,128)}) %reduce-scatter.5.cloned.1.call-update) | async-done | bytes 4718608 | tf_op jit(solution)/shard_map/reduce_scatter | solution.py:71
  (26 shorter events, 1.5 us)
Async XLA Ops:
  7.2 60.5 %all-gather.2.cloned.1.call-start = ((), (), s32[]{:S(2)}) async-start(), calls=%async_computation.3 | async-start | bytes 3342336 | tf_op jit(solution)/shard_map/all_gather | solution.py:55
  7.2 7.1 %collective-permute-start.2 = (bf16[1,1,256,128]{3,2,1,0:T(8,128)(2,1)}, bf16[1,1,256,128]{3,2,1,0:T(8,128)(2,1)S(1)}, u32[]{:S(2)}, u32[]{:S(2)}) collective-permute-start(bf16[1,1,256,128]{3,2,1,0:T(8,128)(2,1)} %param.5), channel_id=1, source_target_pairs={{0,1},{2,3},{4,5},{6,7},{8,9},{10,11},{12,13},{14,15},{16,17},{18,... | collective-permute-start | bytes 196616 | tf_op jit(solution)/shard_map/ppermute | solution.py:14
  12.1 6.4 %collective-permute-start.3 = (bf16[1,1,256,128]{3,2,1,0:T(8,128)(2,1)}, bf16[1,1,256,128]{3,2,1,0:T(8,128)(2,1)S(1)}, u32[]{:S(2)}, u32[]{:S(2)}) collective-permute-start(bf16[1,1,256,128]{3,2,1,0:T(8,128)(2,1)} %param.5), channel_id=1, source_target_pairs={{1,0},{3,2},{5,4},{7,6},{9,8},{11,10},{13,12},{15,14},{17,16},{19,... | collective-permute-start | bytes 196616 | tf_op jit(solution)/shard_map/ppermute | solution.py:15
  20.0 111.2 %reduce-scatter.3.cloned.1.call-start = ((), (), s32[]{:S(2)}) async-start(), calls=%async_computation.2 | async-start | bytes 2228224 | tf_op jit(solution)/shard_map/reduce_scatter | solution.py:46
  20.1 3.9 %collective-permute-start = (bf16[1,1,256,128]{3,2,1,0:T(8,128)(2,1)}, bf16[1,1,256,128]{3,2,1,0:T(8,128)(2,1)S(1)}, u32[]{:S(2)}, u32[]{:S(2)}) collective-permute-start(bf16[1,1,256,128]{3,2,1,0:T(8,128)(2,1)} %param.3), channel_id=1, source_target_pairs={{0,1},{2,3},{4,5},{6,7},{8,9},{10,11},{12,13},{14,15},{16,17},{18,... | collective-permute-start | bytes 196616 | tf_op jit(solution)/shard_map/ppermute | solution.py:14
  21.8 6.4 %collective-permute-start.1 = (bf16[1,1,256,128]{3,2,1,0:T(8,128)(2,1)}, bf16[1,1,256,128]{3,2,1,0:T(8,128)(2,1)S(1)}, u32[]{:S(2)}, u32[]{:S(2)}) collective-permute-start(bf16[1,1,256,128]{3,2,1,0:T(8,128)(2,1)} %param.3), channel_id=1, source_target_pairs={{1,0},{3,2},{5,4},{7,6},{9,8},{11,10},{13,12},{15,14},{17,16},{19,... | collective-permute-start | bytes 196616 | tf_op jit(solution)/shard_map/ppermute | solution.py:15
  35.4 208.4 %reduce-scatter.5.cloned.1.call-start = ((), (), s32[]{:S(2)}) async-start(), calls=%async_computation.4 | async-start | bytes 14155776 | tf_op jit(solution)/shard_map/reduce_scatter | solution.py:71
  74.0 58.7 %copy-start = (bf16[1,3,256,2048]{3,2,1,0:T(8,128)(2,1)S(1)}, bf16[1,3,256,2048]{3,2,1,0:T(8,128)(2,1)}, u32[]{:S(2)}) copy-start(bf16[1,3,256,2048]{3,2,1,0:T(8,128)(2,1)} %all-gather.2.cloned.1.call-done) | copy-start | bytes 9437188
  133.6 2.2 slice-start
  133.9 2.0 slice-start.1
Sparse Core Ops, SparseCore 0:
  20.1 47.4 all-gather.1
  71.4 59.7 reduce-scatter.2
  134.2 109.5 reduce-scatter.4
where the time goes:
time: 251 us; the launch traced here: 250 us
  waiting for transfers between devices  192 us (76%)
  local copies, waits for them, and re-layouts  16.1 us (6%)
  matrix products  14.8 us (6%)
  between operations  13.9 us (6%)
  starting transfers between devices  9.26 us (4%)
  other arithmetic  3.98 us (2%)
    reduce_scatter x1, waiting for transfers between devices, on_device(): lax.psum_scatter(scaled, 'rows', scatter_dimension=3, tiled=True)  105 us
    reduce_scatter x1, waiting for transfers between devices, on_device(): lax.psum_scatter(lax.dot_general(block, columns, contract_first, preferre...  45.3 us
    all_gather x1, waiting for transfers between devices, on_device(): piece = lax.all_gather(grad_rimmed, 'chan', axis=3, tiled=True)  32.2 us
    unnamed x23, local copies, waits for them, and re-layouts  10.8 us
    ppermute x2, waiting for transfers between devices, with_halo(): after = lax.ppermute(initial, axis, down)  8.34 us
    ppermute x2, starting transfers between devices, with_halo(): before = lax.ppermute(last, axis, up)  6.55 us
    dot_general x1, matrix products, on_device(): lax.dot_general(columns, inner, (((0,), (0,)), ((), ())), preferred_eleme...  6.29 us
    dot_general x1, matrix products, on_device(): lax.dot_general(block, columns, contract_first, preferred_element_type=jn...  5.22 us
  transfers between devices with their start and end apart: 7, of which 7 were waited for; matrix products, arithmetic and copies ran while one was open for 13% of the time, Pallas kernels for 0%

commit v1 on v0

--- a/solution.py
+++ b/solution.py
@@ -2,6 +2,30 @@
 import jax.numpy as jnp
 from jax import lax
 from jax.sharding import PartitionSpec as P
+
+
+def create_kinds(mine_x, row_axis):
+    step_out, value_now, tall = (lax.axis_size(row_axis), lax.axis_index(row_axis), mine_x.shape[3])
+    so_far_all = [to_i * step_out if dev == 3 else to_i for dev, to_i in enumerate(mine_x.shape)]
+    block_next = lax.dynamic_update_slice_in_dim(
+        jnp.zeros(so_far_all, mine_x.dtype), mine_x, value_now * tall, axis=3
+    )
+    v_next = extra = mine_x
+    for ii in range(1, step_out // 2 + 1):
+        v_next = lax.ppermute(
+            v_next, row_axis, list(map(lambda dev: (dev, (dev + 1) % step_out), range(step_out)))
+        )
+        block_next = lax.dynamic_update_slice_in_dim(
+            block_next, v_next, (value_now - ii) % step_out * tall, axis=3
+        )
+        if 2 * ii < step_out:
+            extra = lax.ppermute(
+                extra, row_axis, list(map(lambda dev: (dev, (dev - 1) % step_out), range(step_out)))
+            )
+            block_next = lax.dynamic_update_slice_in_dim(
+                block_next, extra, (value_now + ii) % step_out * tall, axis=3
+            )
+    return block_next
 
 
 def with_halo(array, sides, width):
@@ -52,7 +76,7 @@
     outputs = conv_out.T.reshape(batches, height, breadth, local_ch).astype(jnp.bfloat16)
     grad_rimmed = with_halo(cotangent, (("rows", 1),), 1)
     flipped = jnp.transpose(weights[::-1, ::-1], (2, 0, 1, 3))
-    piece = lax.all_gather(grad_rimmed, "chan", axis=3, tiled=True)
+    piece = create_kinds(grad_rimmed, "chan")
     count = piece.shape[3]
     grad_cols = unfold(pad_columns(piece), height, breadth)
     block = flipped.reshape(local_ch, 9 * count)

time: 251 us -> 221 us (0.88)
  waiting for transfers between devices: 192 us -> 130 us
  starting transfers between devices: 9.26 us -> 41 us
  local copies, waits for them, and re-layouts: 16.1 us -> 19 us
    reduce_scatter x1, waiting for transfers between devices: 45.3 us -> 0.01 us  [on_device(): lax.psum_scatter(lax.dot_general(block, columns, contract_first, preferre...]
    ppermute x0 -> x15, waiting for transfers between devices: none -> 33.2 us  [the longest x8 30.8 us: create_kinds(): lax.ppermute(v_next, row_axis, list(map(lambda dev: (dev, (dev + 1) % ste...]
    all_gather x1 -> x0, waiting for transfers between devices: 32.2 us -> none  [on_device(): piece = lax.all_gather(grad_rimmed, 'chan', axis=3, tiled=True)]
    ppermute x0 -> x15, starting transfers between devices: none -> 31.8 us  [the longest x7 31.7 us: create_kinds(): lax.ppermute(extra, row_axis, list(map(lambda dev: (dev, (dev - 1) % step...]
    reduce_scatter x1, waiting for transfers between devices: 105 us -> 87.3 us  [on_device(): lax.psum_scatter(scaled, 'rows', scatter_dimension=3, tiled=True)]
    unnamed x23 -> x29, local copies, waits for them, and re-layouts: 10.8 us -> 11.6 us
  transfers between devices with their start and end apart: 7 -> 21, of which waited for: 7 -> 15; matrix products, arithmetic and copies ran while one was open for 13% -> 12% of each run, Pallas kernels for 0% -> 0%
where the time goes in v1:
time: 221 us
  waiting for transfers between devices  130 us (59%)
  starting transfers between devices  41 us (19%)
  local copies, waits for them, and re-layouts  19 us (9%)
  between operations  14.4 us (7%)
  matrix products  13.6 us (6%)
  other arithmetic  2.47 us (1%)
    reduce_scatter x1, waiting for transfers between devices, on_device(): lax.psum_scatter(scaled, 'rows', scatter_dimension=3, tiled=True)  87.3 us
    ppermute x7, starting transfers between devices, create_kinds(): lax.ppermute(extra, row_axis, list(map(lambda dev: (dev, (dev - 1) % step...  31.7 us
    ppermute x8, waiting for transfers between devices, create_kinds(): lax.ppermute(v_next, row_axis, list(map(lambda dev: (dev, (dev + 1) % ste...  30.8 us
    unnamed x29, local copies, waits for them, and re-layouts  11.6 us
    ppermute x2, waiting for transfers between devices, with_halo(): after = lax.ppermute(initial, axis, down)  8.43 us
    ppermute x2, starting transfers between devices, with_halo(): before = lax.ppermute(last, axis, up)  6.56 us
    dot_general x1, matrix products, on_device(): lax.dot_general(block, columns, contract_first, preferred_element_type=jn...  5.25 us
    dot_general x1, matrix products, on_device(): lax.dot_general(columns, inner, (((0,), (0,)), ((), ())), preferred_eleme...  5.1 us
  transfers between devices with their start and end apart: 21, of which 15 were waited for; matrix products, arithmetic and copies ran while one was open for 12% of the time, Pallas kernels for 0%

profile of v1, /device:TPU:0, one launch (start us, length us, event | category | flops | bytes accessed | tf_op | source)
XLA Modules:
  0.0 220.9 jit_solution(6798835909079258797)
XLA Ops:
  7.2 4.9 %collective-permute-start = (bf16[1,1,256,128]{3,2,1,0:T(8,128)(2,1)}, bf16[1,1,256,128]{3,2,1,0:T(8,128)(2,1)S(1)}, u32[]{:S(2)}, u32[]{:S(2)}) collective-permute-start(bf16[1,1,256,128]{3,2,1,0:T(8,128)(2,1)} %param.3), channel_id=1, source_target_pairs={{0,1},{2,3},{4,5},{6,7},{8,9},{10,11},{12,13},{14,15},{16,17},{18,... | collective-permute-start | bytes 196616 | tf_op jit(solution)/shard_map/ppermute | solution.py:38
  14.3 4.2 %collective-permute-done.1 = bf16[1,1,256,128]{3,2,1,0:T(8,128)(2,1)S(1)} collective-permute-done((bf16[1,1,256,128]{3,2,1,0:T(8,128)(2,1)}, bf16[1,1,256,128]{3,2,1,0:T(8,128)(2,1)S(1)}, u32[]{:S(2)}, u32[]{:S(2)}) %collective-permute-start.1) | collective-permute-done | bytes 65568 | tf_op jit(solution)/shard_map/ppermute | solution.py:39
  21.3 5.2 %convolution_bitcast_fusion = f32[2048,256]{0,1:T(8,128)} fusion(bf16[1152,2048]{1,0:T(8,128)(2,1)} %bitcast.34, bf16[1,1,256,1152]{3,2,1,0:T(8,128)(2,1)S(1)} %slice_dynamic-update-slice_fusion.3), kind=kOutput, calls=%fused_computation.3 | convolution fusion | flops 1207959552 | bytes 7405568 | tf_op jit(solution)/shard_map/dot_general | solution.py:71
  30.2 4.3 %collective-permute-done.3 = bf16[1,1,256,128]{3,2,1,0:T(8,128)(2,1)S(1)} collective-permute-done((bf16[1,1,256,128]{3,2,1,0:T(8,128)(2,1)S(1)}, bf16[1,1,256,128]{3,2,1,0:T(8,128)(2,1)S(1)}, u32[]{:S(2)}, u32[]{:S(2)}) %collective-permute-start.3) | collective-permute-done | bytes 65568 | tf_op jit(solution)/shard_map/ppermute | solution.py:39
  34.5 4.4 %collective-permute-start.5 = (bf16[1,3,256,128]{3,2,1,0:T(8,128)(2,1)S(1)}, bf16[1,3,256,128]{3,2,1,0:T(8,128)(2,1)S(1)}, u32[]{:S(2)}, u32[]{:S(2)}) collective-permute-start(bf16[1,3,256,128]{3,2,1,0:T(8,128)(2,1)S(1)} %constant_dynamic-update-slice_fusion.3), channel_id=1, source_target_pairs={{0,30},{2,0},{4,2},{6,4},{8,6},{10,8},{12,10},{14,12},{16,14},{18,... | collective-permute-start | bytes 589832 | tf_op jit(solution)/shard_map/ppermute | solution.py:22
  39.4 3.1 %collective-permute-done.4 = bf16[1,3,256,128]{3,2,1,0:T(8,128)(2,1)} collective-permute-done((bf16[1,3,256,128]{3,2,1,0:T(8,128)(2,1)S(1)}, bf16[1,3,256,128]{3,2,1,0:T(8,128)(2,1)}, u32[]{:S(2)}, u32[]{:S(2)}) %collective-permute-start.4) | collective-permute-done | bytes 196640 | tf_op jit(solution)/shard_map/ppermute | solution.py:15
  42.5 4.4 %collective-permute-start.7 = (bf16[1,3,256,128]{3,2,1,0:T(8,128)(2,1)S(1)}, bf16[1,3,256,128]{3,2,1,0:T(8,128)(2,1)S(1)}, u32[]{:S(2)}, u32[]{:S(2)}) collective-permute-start(bf16[1,3,256,128]{3,2,1,0:T(8,128)(2,1)S(1)} %collective-permute-done.5), channel_id=1, source_target_pairs={{0,30},{2,0},{4,2},{6,4},{8,6},{10,8},{12,10},{14,12},{16,14},{18,... | collective-permute-start | bytes 589832 | tf_op jit(solution)/shard_map/ppermute | solution.py:22
  48.0 2.6 %collective-permute-done.6 = bf16[1,3,256,128]{3,2,1,0:T(8,128)(2,1)S(1)} collective-permute-done((bf16[1,3,256,128]{3,2,1,0:T(8,128)(2,1)}, bf16[1,3,256,128]{3,2,1,0:T(8,128)(2,1)S(1)}, u32[]{:S(2)}, u32[]{:S(2)}) %collective-permute-start.6) | collective-permute-done | bytes 196640 | tf_op jit(solution)/shard_map/ppermute | solution.py:15
  50.7 4.4 %collective-permute-start.9 = (bf16[1,3,256,128]{3,2,1,0:T(8,128)(2,1)S(1)}, bf16[1,3,256,128]{3,2,1,0:T(8,128)(2,1)S(1)}, u32[]{:S(2)}, u32[]{:S(2)}) collective-permute-start(bf16[1,3,256,128]{3,2,1,0:T(8,128)(2,1)S(1)} %collective-permute-done.7), channel_id=1, source_target_pairs={{0,30},{2,0},{4,2},{6,4},{8,6},{10,8},{12,10},{14,12},{16,14},{18,... | collective-permute-start | bytes 589832 | tf_op jit(solution)/shard_map/ppermute | solution.py:22
  55.2 3.3 %collective-permute-done.8 = bf16[1,3,256,128]{3,2,1,0:T(8,128)(2,1)S(1)} collective-permute-done((bf16[1,3,256,128]{3,2,1,0:T(8,128)(2,1)S(1)}, bf16[1,3,256,128]{3,2,1,0:T(8,128)(2,1)S(1)}, u32[]{:S(2)}, u32[]{:S(2)}) %collective-permute-start.8) | collective-permute-done | bytes 196640 | tf_op jit(solution)/shard_map/ppermute | solution.py:15
  59.7 4.7 %collective-permute-start.11 = (bf16[1,3,256,128]{3,2,1,0:T(8,128)(2,1)S(1)}, bf16[1,3,256,128]{3,2,1,0:T(8,128)(2,1)S(1)}, u32[]{:S(2)}, u32[]{:S(2)}) collective-permute-start(bf16[1,3,256,128]{3,2,1,0:T(8,128)(2,1)S(1)} %collective-permute-done.9), channel_id=1, source_target_pairs={{0,30},{2,0},{4,2},{6,4},{8,6},{10,8},{12,10},{14,12},{16,14},{18,... | collective-permute-start | bytes 589832 | tf_op jit(solution)/shard_map/ppermute | solution.py:22
  64.5 2.5 %collective-permute-done.10 = bf16[1,3,256,128]{3,2,1,0:T(8,128)(2,1)S(1)} collective-permute-done((bf16[1,3,256,128]{3,2,1,0:T(8,128)(2,1)S(1)}, bf16[1,3,256,128]{3,2,1,0:T(8,128)(2,1)S(1)}, u32[]{:S(2)}, u32[]{:S(2)}) %collective-permute-start.10) | collective-permute-done | bytes 196640 | tf_op jit(solution)/shard_map/ppermute | solution.py:15
  68.3 4.7 %collective-permute-start.13 = (bf16[1,3,256,128]{3,2,1,0:T(8,128)(2,1)S(1)}, bf16[1,3,256,128]{3,2,1,0:T(8,128)(2,1)S(1)}, u32[]{:S(2)}, u32[]{:S(2)}) collective-permute-start(bf16[1,3,256,128]{3,2,1,0:T(8,128)(2,1)S(1)} %collective-permute-done.11), channel_id=1, source_target_pairs={{0,30},{2,0},{4,2},{6,4},{8,6},{10,8},{12,10},{14,12},{16,14},{18,... | collective-permute-start | bytes 589832 | tf_op jit(solution)/shard_map/ppermute | solution.py:22
  73.2 3.5 %collective-permute-done.12 = bf16[1,3,256,128]{3,2,1,0:T(8,128)(2,1)S(1)} collective-permute-done((bf16[1,3,256,128]{3,2,1,0:T(8,128)(2,1)S(1)}, bf16[1,3,256,128]{3,2,1,0:T(8,128)(2,1)S(1)}, u32[]{:S(2)}, u32[]{:S(2)}) %collective-permute-start.12) | collective-permute-done | bytes 196640 | tf_op jit(solution)/shard_map/ppermute | solution.py:15
  76.7 4.4 %collective-permute-start.15 = (bf16[1,3,256,128]{3,2,1,0:T(8,128)(2,1)S(1)}, bf16[1,3,256,128]{3,2,1,0:T(8,128)(2,1)S(1)}, u32[]{:S(2)}, u32[]{:S(2)}) collective-permute-start(bf16[1,3,256,128]{3,2,1,0:T(8,128)(2,1)S(1)} %collective-permute-done.13), channel_id=1, source_target_pairs={{0,30},{2,0},{4,2},{6,4},{8,6},{10,8},{12,10},{14,12},{16,14},{18,... | collective-permute-start | bytes 589832 | tf_op jit(solution)/shard_map/ppermute | solution.py:22
  81.3 3.4 %collective-permute-done.14 = bf16[1,3,256,128]{3,2,1,0:T(8,128)(2,1)S(1)} collective-permute-done((bf16[1,3,256,128]{3,2,1,0:T(8,128)(2,1)S(1)}, bf16[1,3,256,128]{3,2,1,0:T(8,128)(2,1)S(1)}, u32[]{:S(2)}, u32[]{:S(2)}) %collective-permute-start.14) | collective-permute-done | bytes 196640 | tf_op jit(solution)/shard_map/ppermute | solution.py:15
  84.6 4.5 %collective-permute-start.17 = (bf16[1,3,256,128]{3,2,1,0:T(8,128)(2,1)S(1)}, bf16[1,3,256,128]{3,2,1,0:T(8,128)(2,1)S(1)}, u32[]{:S(2)}, u32[]{:S(2)}) collective-permute-start(bf16[1,3,256,128]{3,2,1,0:T(8,128)(2,1)S(1)} %collective-permute-done.15), channel_id=1, source_target_pairs={{0,30},{2,0},{4,2},{6,4},{8,6},{10,8},{12,10},{14,12},{16,14},{18,... | collective-permute-start | bytes 589832 | tf_op jit(solution)/shard_map/ppermute | solution.py:22
  89.3 4.8 %collective-permute-done.16 = bf16[1,3,256,128]{3,2,1,0:T(8,128)(2,1)S(1)} collective-permute-done((bf16[1,3,256,128]{3,2,1,0:T(8,128)(2,1)S(1)}, bf16[1,3,256,128]{3,2,1,0:T(8,128)(2,1)S(1)}, u32[]{:S(2)}, u32[]{:S(2)}) %collective-permute-start.16) | collective-permute-done | bytes 196640 | tf_op jit(solution)/shard_map/ppermute | solution.py:15
  94.3 7.6 %collective-permute-done.18 = bf16[1,3,256,128]{3,2,1,0:T(8,128)(2,1)S(1)} collective-permute-done((bf16[1,3,256,128]{3,2,1,0:T(8,128)(2,1)S(1)}, bf16[1,3,256,128]{3,2,1,0:T(8,128)(2,1)S(1)}, u32[]{:S(2)}, u32[]{:S(2)}) %collective-permute-start.18) | collective-permute-done | bytes 196640 | tf_op jit(solution)/shard_map/ppermute | solution.py:15
  102.0 5.1 %convolution_multiply_fusion = f32[1152,2048]{1,0:T(8,128)} fusion(bf16[1,3,256,2048]{3,2,1,0:T(8,128)(2,1)S(1)} %constant_dynamic-update-slice_fusion.6, bf16[1,1,256,1152]{3,2,1,0:T(8,128)(2,1)S(1)} %copy-done.1), kind=kOutput, calls=%fused_computation | convolution fusion | flops 1210318848 | bytes 11075584 | tf_op jit(solution)/shard_map/dot_general | solution.py:87
  107.1 6.8 %copy.6 = bf16[3,3,128,2048]{2,3,1,0:T(8,128)(2,1)} copy(bf16[3,3,128,2048]{3,2,1,0:T(8,128)(2,1)} %param.4) | data formatting | bytes 9437184 | tf_op args[1]
  113.9 4.7 %rev.3 = bf16[3,3,128,2048]{2,3,1,0:T(8,128)(2,1)} reverse(bf16[3,3,128,2048]{2,3,1,0:T(8,128)(2,1)} %copy.6), dimensions={0,1} | reverse | bytes 9437184 | tf_op jit(solution)/shard_map/rev | solution.py:78
  122.0 3.2 %fusion.5 = bf16[1,1,256,128]{3,2,1,0:T(8,128)(2,1)} fusion(bf16[128,18432]{0,1:T(8,128)(2,1)S(1)} %bitcast.33, bf16[1,1,256,18432]{3,2,1,0:T(8,128)(2,1)S(1)} %fusion.13), kind=kOutput, calls=%fused_computation.11 | convolution fusion | flops 1207992320 | bytes 14221312 | tf_op jit(solution)/shard_map/dot_general | solution.py:83
  126.8 87.3 %reduce-scatter.5.cloned.1.call-done = f32[3,3,128,1024]{3,2,1,0:T(8,128)} async-done(((f32[3,3,128,2048]{3,2,1,0:T(8,128)}), f32[3,3,128,1024]{3,2,1,0:T(8,128)}) %reduce-scatter.5.cloned.1.call-update) | async-done | bytes 4718608 | tf_op jit(solution)/shard_map/reduce_scatter | solution.py:95
  (76 shorter events, 18.3 us)
Async XLA Ops:
  7.2 118.0 %reduce-scatter.3.cloned.1.call-start = ((), (), s32[]{:S(2)}) async-start(), calls=%async_computation.2 | async-start | bytes 2228224 | tf_op jit(solution)/shard_map/reduce_scatter | solution.py:70
  7.2 7.1 %collective-permute-start = (bf16[1,1,256,128]{3,2,1,0:T(8,128)(2,1)}, bf16[1,1,256,128]{3,2,1,0:T(8,128)(2,1)S(1)}, u32[]{:S(2)}, u32[]{:S(2)}) collective-permute-start(bf16[1,1,256,128]{3,2,1,0:T(8,128)(2,1)} %param.3), channel_id=1, source_target_pairs={{0,1},{2,3},{4,5},{6,7},{8,9},{10,11},{12,13},{14,15},{16,17},{18,... | collective-permute-start | bytes 196616 | tf_op jit(solution)/shard_map/ppermute | solution.py:38
  12.1 6.4 %collective-permute-start.1 = (bf16[1,1,256,128]{3,2,1,0:T(8,128)(2,1)}, bf16[1,1,256,128]{3,2,1,0:T(8,128)(2,1)S(1)}, u32[]{:S(2)}, u32[]{:S(2)}) collective-permute-start(bf16[1,1,256,128]{3,2,1,0:T(8,128)(2,1)} %param.3), channel_id=1, source_target_pairs={{1,0},{3,2},{5,4},{7,6},{9,8},{11,10},{13,12},{15,14},{17,16},{19,... | collective-permute-start | bytes 196616 | tf_op jit(solution)/shard_map/ppermute | solution.py:39
  21.3 5.3 %copy-start.2 = (bf16[1,1,256,128]{3,2,1,0:T(8,128)(2,1)S(1)}, bf16[1,1,256,128]{3,2,1,0:T(8,128)(2,1)}, u32[]{:S(2)}) copy-start(bf16[1,1,256,128]{3,2,1,0:T(8,128)(2,1)} %param.5) | copy-start | bytes 196612
  26.6 187.5 %reduce-scatter.5.cloned.1.call-start = ((), (), s32[]{:S(2)}) async-start(), calls=%async_computation.3 | async-start | bytes 14155776 | tf_op jit(solution)/shard_map/reduce_scatter | solution.py:95
  26.6 3.6 %collective-permute-start.2 = (bf16[1,1,256,128]{3,2,1,0:T(8,128)(2,1)S(1)}, bf16[1,1,256,128]{3,2,1,0:T(8,128)(2,1)S(1)}, u32[]{:S(2)}, u32[]{:S(2)}) collective-permute-start(bf16[1,1,256,128]{3,2,1,0:T(8,128)(2,1)S(1)} %copy-done.2), channel_id=1, source_target_pairs={{0,1},{2,3},{4,5},{6,7},{8,9},{10,11},{12,13},{14,15},{16,17},{18,... | collective-permute-start | bytes 196616 | tf_op jit(solution)/shard_map/ppermute | solution.py:38
  28.3 6.2 %collective-permute-start.3 = (bf16[1,1,256,128]{3,2,1,0:T(8,128)(2,1)S(1)}, bf16[1,1,256,128]{3,2,1,0:T(8,128)(2,1)S(1)}, u32[]{:S(2)}, u32[]{:S(2)}) collective-permute-start(bf16[1,1,256,128]{3,2,1,0:T(8,128)(2,1)S(1)} %copy-done.2), channel_id=1, source_target_pairs={{1,0},{3,2},{5,4},{7,6},{9,8},{11,10},{13,12},{15,14},{17,16},{19,... | collective-permute-start | bytes 196616 | tf_op jit(solution)/shard_map/ppermute | solution.py:39
  34.5 8.1 %collective-permute-start.4 = (bf16[1,3,256,128]{3,2,1,0:T(8,128)(2,1)S(1)}, bf16[1,3,256,128]{3,2,1,0:T(8,128)(2,1)}, u32[]{:S(2)}, u32[]{:S(2)}) collective-permute-start(bf16[1,3,256,128]{3,2,1,0:T(8,128)(2,1)S(1)} %constant_dynamic-update-slice_fusion.3), channel_id=1, source_target_pairs={{0,2},{2,4},{4,6},{6,8},{8,10},{10,12},{12,14},{14,16},{16,18},{18... | collective-permute-start | bytes 589832 | tf_op jit(solution)/shard_map/ppermute | solution.py:15
  34.5 8.0 %collective-permute-start.5 = (bf16[1,3,256,128]{3,2,1,0:T(8,128)(2,1)S(1)}, bf16[1,3,256,128]{3,2,1,0:T(8,128)(2,1)S(1)}, u32[]{:S(2)}, u32[]{:S(2)}) collective-permute-start(bf16[1,3,256,128]{3,2,1,0:T(8,128)(2,1)S(1)} %constant_dynamic-update-slice_fusion.3), channel_id=1, source_target_pairs={{0,30},{2,0},{4,2},{6,4},{8,6},{10,8},{12,10},{14,12},{16,14},{18,... | collective-permute-start | bytes 589832 | tf_op jit(solution)/shard_map/ppermute | solution.py:22
  39.4 62.6 %copy-start.1 = (bf16[1,1,256,1152]{3,2,1,0:T(8,128)(2,1)S(1)}, bf16[1,1,256,1152]{3,2,1,0:T(8,128)(2,1)}, u32[]{:S(2)}) copy-start(bf16[1,1,256,1152]{3,2,1,0:T(8,128)(2,1)} %copy-done) | copy-start | bytes 1769476
  42.5 8.1 %collective-permute-start.6 = (bf16[1,3,256,128]{3,2,1,0:T(8,128)(2,1)}, bf16[1,3,256,128]{3,2,1,0:T(8,128)(2,1)S(1)}, u32[]{:S(2)}, u32[]{:S(2)}) collective-permute-start(bf16[1,3,256,128]{3,2,1,0:T(8,128)(2,1)} %collective-permute-done.4), channel_id=1, source_target_pairs={{0,2},{2,4},{4,6},{6,8},{8,10},{10,12},{12,14},{14,16},{16,18},{18... | collective-permute-start | bytes 589832 | tf_op jit(solution)/shard_map/ppermute | solution.py:15
  42.5 8.1 %collective-permute-start.7 = (bf16[1,3,256,128]{3,2,1,0:T(8,128)(2,1)S(1)}, bf16[1,3,256,128]{3,2,1,0:T(8,128)(2,1)S(1)}, u32[]{:S(2)}, u32[]{:S(2)}) collective-permute-start(bf16[1,3,256,128]{3,2,1,0:T(8,128)(2,1)S(1)} %collective-permute-done.5), channel_id=1, source_target_pairs={{0,30},{2,0},{4,2},{6,4},{8,6},{10,8},{12,10},{14,12},{16,14},{18,... | collective-permute-start | bytes 589832 | tf_op jit(solution)/shard_map/ppermute | solution.py:22
  50.6 7.9 %collective-permute-start.8 = (bf16[1,3,256,128]{3,2,1,0:T(8,128)(2,1)S(1)}, bf16[1,3,256,128]{3,2,1,0:T(8,128)(2,1)S(1)}, u32[]{:S(2)}, u32[]{:S(2)}) collective-permute-start(bf16[1,3,256,128]{3,2,1,0:T(8,128)(2,1)S(1)} %collective-permute-done.6), channel_id=1, source_target_pairs={{0,2},{2,4},{4,6},{6,8},{8,10},{10,12},{12,14},{14,16},{16,18},{18... | collective-permute-start | bytes 589832 | tf_op jit(solution)/shard_map/ppermute | solution.py:15
  50.7 9.0 %collective-permute-start.9 = (bf16[1,3,256,128]{3,2,1,0:T(8,128)(2,1)S(1)}, bf16[1,3,256,128]{3,2,1,0:T(8,128)(2,1)S(1)}, u32[]{:S(2)}, u32[]{:S(2)}) collective-permute-start(bf16[1,3,256,128]{3,2,1,0:T(8,128)(2,1)S(1)} %collective-permute-done.7), channel_id=1, source_target_pairs={{0,30},{2,0},{4,2},{6,4},{8,6},{10,8},{12,10},{14,12},{16,14},{18,... | collective-permute-start | bytes 589832 | tf_op jit(solution)/shard_map/ppermute | solution.py:22
  58.6 8.5 %collective-permute-start.10 = (bf16[1,3,256,128]{3,2,1,0:T(8,128)(2,1)S(1)}, bf16[1,3,256,128]{3,2,1,0:T(8,128)(2,1)S(1)}, u32[]{:S(2)}, u32[]{:S(2)}) collective-permute-start(bf16[1,3,256,128]{3,2,1,0:T(8,128)(2,1)S(1)} %collective-permute-done.8), channel_id=1, source_target_pairs={{0,2},{2,4},{4,6},{6,8},{8,10},{10,12},{12,14},{14,16},{16,18},{18... | collective-permute-start | bytes 589832 | tf_op jit(solution)/shard_map/ppermute | solution.py:15
  59.7 8.6 %collective-permute-start.11 = (bf16[1,3,256,128]{3,2,1,0:T(8,128)(2,1)S(1)}, bf16[1,3,256,128]{3,2,1,0:T(8,128)(2,1)S(1)}, u32[]{:S(2)}, u32[]{:S(2)}) collective-permute-start(bf16[1,3,256,128]{3,2,1,0:T(8,128)(2,1)S(1)} %collective-permute-done.9), channel_id=1, source_target_pairs={{0,30},{2,0},{4,2},{6,4},{8,6},{10,8},{12,10},{14,12},{16,14},{18,... | collective-permute-start | bytes 589832 | tf_op jit(solution)/shard_map/ppermute | solution.py:22
  67.0 9.7 %collective-permute-start.12 = (bf16[1,3,256,128]{3,2,1,0:T(8,128)(2,1)S(1)}, bf16[1,3,256,128]{3,2,1,0:T(8,128)(2,1)S(1)}, u32[]{:S(2)}, u32[]{:S(2)}) collective-permute-start(bf16[1,3,256,128]{3,2,1,0:T(8,128)(2,1)S(1)} %collective-permute-done.10), channel_id=1, source_target_pairs={{0,2},{2,4},{4,6},{6,8},{8,10},{10,12},{12,14},{14,16},{16,18},{18... | collective-permute-start | bytes 589832 | tf_op jit(solution)/shard_map/ppermute | solution.py:15
  68.3 8.4 %collective-permute-start.13 = (bf16[1,3,256,128]{3,2,1,0:T(8,128)(2,1)S(1)}, bf16[1,3,256,128]{3,2,1,0:T(8,128)(2,1)S(1)}, u32[]{:S(2)}, u32[]{:S(2)}) collective-permute-start(bf16[1,3,256,128]{3,2,1,0:T(8,128)(2,1)S(1)} %collective-permute-done.11), channel_id=1, source_target_pairs={{0,30},{2,0},{4,2},{6,4},{8,6},{10,8},{12,10},{14,12},{16,14},{18,... | collective-permute-start | bytes 589832 | tf_op jit(solution)/shard_map/ppermute | solution.py:22
  76.7 7.9 %collective-permute-start.14 = (bf16[1,3,256,128]{3,2,1,0:T(8,128)(2,1)S(1)}, bf16[1,3,256,128]{3,2,1,0:T(8,128)(2,1)S(1)}, u32[]{:S(2)}, u32[]{:S(2)}) collective-permute-start(bf16[1,3,256,128]{3,2,1,0:T(8,128)(2,1)S(1)} %collective-permute-done.12), channel_id=1, source_target_pairs={{0,2},{2,4},{4,6},{6,8},{8,10},{10,12},{12,14},{14,16},{16,18},{18... | collective-permute-start | bytes 589832 | tf_op jit(solution)/shard_map/ppermute | solution.py:15
  76.7 7.9 %collective-permute-start.15 = (bf16[1,3,256,128]{3,2,1,0:T(8,128)(2,1)S(1)}, bf16[1,3,256,128]{3,2,1,0:T(8,128)(2,1)S(1)}, u32[]{:S(2)}, u32[]{:S(2)}) collective-permute-start(bf16[1,3,256,128]{3,2,1,0:T(8,128)(2,1)S(1)} %collective-permute-done.13), channel_id=1, source_target_pairs={{0,30},{2,0},{4,2},{6,4},{8,6},{10,8},{12,10},{14,12},{16,14},{18,... | collective-permute-start | bytes 589832 | tf_op jit(solution)/shard_map/ppermute | solution.py:22
  84.6 9.5 %collective-permute-start.16 = (bf16[1,3,256,128]{3,2,1,0:T(8,128)(2,1)S(1)}, bf16[1,3,256,128]{3,2,1,0:T(8,128)(2,1)S(1)}, u32[]{:S(2)}, u32[]{:S(2)}) collective-permute-start(bf16[1,3,256,128]{3,2,1,0:T(8,128)(2,1)S(1)} %collective-permute-done.14), channel_id=1, source_target_pairs={{0,2},{2,4},{4,6},{6,8},{8,10},{10,12},{12,14},{14,16},{16,18},{18... | collective-permute-start | bytes 589832 | tf_op jit(solution)/shard_map/ppermute | solution.py:15
  84.6 9.6 %collective-permute-start.17 = (bf16[1,3,256,128]{3,2,1,0:T(8,128)(2,1)S(1)}, bf16[1,3,256,128]{3,2,1,0:T(8,128)(2,1)S(1)}, u32[]{:S(2)}, u32[]{:S(2)}) collective-permute-start(bf16[1,3,256,128]{3,2,1,0:T(8,128)(2,1)S(1)} %collective-permute-done.15), channel_id=1, source_target_pairs={{0,30},{2,0},{4,2},{6,4},{8,6},{10,8},{12,10},{14,12},{16,14},{18,... | collective-permute-start | bytes 589832 | tf_op jit(solution)/shard_map/ppermute | solution.py:22
  94.1 7.8 %collective-permute-start.18 = (bf16[1,3,256,128]{3,2,1,0:T(8,128)(2,1)S(1)}, bf16[1,3,256,128]{3,2,1,0:T(8,128)(2,1)S(1)}, u32[]{:S(2)}, u32[]{:S(2)}) collective-permute-start(bf16[1,3,256,128]{3,2,1,0:T(8,128)(2,1)S(1)} %collective-permute-done.16), channel_id=1, source_target_pairs={{0,2},{2,4},{4,6},{6,8},{8,10},{10,12},{12,14},{14,16},{16,18},{18... | collective-permute-start | bytes 589832 | tf_op jit(solution)/shard_map/ppermute | solution.py:15
  119.6 2.2 %slice-start = ((s8[4718592]{0:T(1024)(128)(4,1)}), s8[4194304]{0:T(1024)(128)(4,1)S(1)}, s32[]{:S(2)}) async-start(s8[4718592]{0:T(1024)(128)(4,1)} %bitcast.31), calls=%async_computation.4 | async-start | bytes 8388608
  (2 other events, 2.9 us)
Sparse Core Ops, SparseCore 0:
  26.7 67.6 reduce-scatter.2
  107.2 106.7 reduce-scatter.4
